TPU v7x, 512 devices: a whole 4x8x8 slice. The times are simulated.
512 devices in a mesh: seq: 32 (over x, y_lo, core), chan: 16 (over y_hi, z).
Axes of the slice: x: 4, y: 8 (y_hi: 2, y_lo: 4; y = y_hi * 4 + y_lo), z: 8, core: 2. Of those that a mesh axis runs over, the one named last changes fastest.
Arguments:
- key_value: bfloat16 [16384, 4096], P('seq', 'chan'), may hold values from -6 to 6
- gating: bfloat16 [16384, 4096], P('seq', 'chan'), may hold values from -6 to 6
- long_filter: bfloat16 [16384, 4096], P('seq', 'chan'), may hold values from -0.046875 to 0.046875
- skip_gain: float32 [4096], P('chan'), may hold values from -4 to 4
- out_weight: bfloat16 [4096, 4096], P('chan'), may hold values from -0.125 to 0.125
Outputs:
- mixed: bfloat16 [16384, 4096], P('seq', 'chan')
All inputs are finite; a program needn't handle non-finite values.
Results may differ from a plain program's by a relative error of at most 0.023.
Values may be sent and summed in bfloat16 or wider, within the bound.
A program may use at most 64 MiB of HBM per device.

v0:
```python
import math

import jax
import jax.numpy as jnp
from jax import lax
from jax.sharding import PartitionSpec as P

HIGH = lax.Precision.HIGHEST
TWO_PI = 2.0 * math.pi


def as_sent(array):

    def short(part):
        return part.astype(jnp.bfloat16) if part.dtype == jnp.float32 else part

    return jax.tree.map(short, array)


def phases(rows_index, cols_index, period):
    product = rows_index[:, None] * cols_index[None, :] % period
    return product.astype(jnp.float32) * (TWO_PI / period)


def rotate_sum(real_part, imag_part, cos_table, sin_table, form, sign):

    def contract(values, table):
        return jnp.einsum(form, values, table, precision=HIGH)

    if imag_part is None:
        return (contract(real_part, cos_table), sign * contract(real_part, sin_table))
    new_real = contract(real_part, cos_table) - sign * contract(imag_part, sin_table)
    new_imag = contract(imag_part, cos_table) + sign * contract(real_part, sin_table)
    return (new_real, new_imag)


def twiddle(real_part, imag_part, angle, sign):
    cosine = jnp.cos(angle)
    sine = jnp.sin(angle)
    return (
        real_part * cosine - sign * imag_part * sine,
        imag_part * cosine + sign * real_part * sine,
    )


def spectrum_product(left_real, left_imag, right_real, right_imag):
    return (
        left_real * right_real - left_imag * right_imag,
        left_real * right_imag + left_imag * right_real,
    )


def step_tables(seq_count):
    step_index = jnp.arange(seq_count, dtype=jnp.int32)
    freq_index = jnp.arange(2 * seq_count, dtype=jnp.int32)
    outer = phases(step_index, freq_index, 2 * seq_count)
    return (jnp.cos(outer), jnp.sin(outer))


def block_tables(block):
    positions = jnp.arange(block, dtype=jnp.int32)
    inner = phases(positions, positions, block)
    return (jnp.cos(inner), jnp.sin(inner))


def per_device(key_value, gating, long_filter, skip_gain, out_weight):
    seq_count = lax.axis_size("seq")
    block, chans = key_value.shape
    period = 2 * seq_count * block
    rows_per = block // seq_count
    here = lax.axis_index("seq")
    cos_steps, sin_steps = step_tables(seq_count)
    cos_block, sin_block = block_tables(block)
    freq_index = jnp.arange(2 * seq_count, dtype=jnp.int32)
    positions = jnp.arange(block, dtype=jnp.int32)
    got_signal, got_kernel = (
        lax.all_to_all(
            key_value.reshape(1, block, chans), "seq", split_axis=1, concat_axis=0, tiled=True
        ),
        lax.all_to_all(
            long_filter.reshape(1, block, chans), "seq", split_axis=1, concat_axis=0, tiled=True
        ),
    )
    local_rows = here * rows_per + jnp.arange(rows_per, dtype=jnp.int32)
    spin_first = phases(freq_index, local_rows, period)[:, :, None]

    def first_section(values):
        first_real, first_imag = rotate_sum(
            values.astype(jnp.float32), None, cos_steps, sin_steps, "jrc,jk->krc", -1.0
        )
        return twiddle(first_real, first_imag, spin_first, -1.0)

    sig_real, sig_imag = first_section(got_signal)
    ker_real, ker_imag = first_section(got_kernel)
    left_real = lax.all_to_all(
        sig_real.astype(jnp.bfloat16), "seq", split_axis=0, concat_axis=1, tiled=True
    ).astype(sig_real.dtype)
    left_imag = lax.all_to_all(
        sig_imag.astype(jnp.bfloat16), "seq", split_axis=0, concat_axis=1, tiled=True
    ).astype(sig_imag.dtype)
    right_real = lax.all_to_all(
        ker_real.astype(jnp.bfloat16), "seq", split_axis=0, concat_axis=1, tiled=True
    ).astype(ker_real.dtype)
    right_imag = lax.all_to_all(
        ker_imag.astype(jnp.bfloat16), "seq", split_axis=0, concat_axis=1, tiled=True
    ).astype(ker_imag.dtype)
    freq_local = left_real.shape[0]
    sig_freq = rotate_sum(left_real, left_imag, cos_block, sin_block, "krc,rm->kmc", -1.0)
    ker_freq = rotate_sum(right_real, right_imag, cos_block, sin_block, "krc,rm->kmc", -1.0)
    prod_real, prod_imag = spectrum_product(sig_freq[0], sig_freq[1], ker_freq[0], ker_freq[1])
    back_real, back_imag = rotate_sum(
        prod_real, prod_imag, cos_block, sin_block, "kmc,mr->krc", 1.0
    )
    owned_freq = here * freq_local + jnp.arange(freq_local, dtype=jnp.int32)
    spin_back = phases(owned_freq, positions, period)[:, :, None]
    back_real, back_imag = twiddle(back_real, back_imag, spin_back, 1.0)
    mid_real = lax.all_to_all(
        as_sent(back_real), "seq", split_axis=1, concat_axis=0, tiled=True
    ).astype(back_real.dtype)
    mid_imag = lax.all_to_all(
        as_sent(back_imag), "seq", split_axis=1, concat_axis=0, tiled=True
    ).astype(back_imag.dtype)
    rows_values = jnp.einsum("krc,jk->jrc", mid_real, cos_steps, precision=HIGH)
    rows_values = (
        rows_values - jnp.einsum("krc,jk->jrc", mid_imag, sin_steps, precision=HIGH)
    ) / period
    conv = (
        lax.all_to_all(as_sent(rows_values), "seq", split_axis=0, concat_axis=1, tiled=True)
        .astype(rows_values.dtype)
        .reshape(block, chans)
    )
    gated = (
        gating.astype(jnp.float32) * (conv + skip_gain[None, :] * key_value.astype(jnp.float32))
    ).astype(jnp.bfloat16)
    partial_sums = jnp.dot(gated, out_weight, preferred_element_type=jnp.float32)
    return lax.psum_scatter(
        partial_sums.astype(jnp.bfloat16), "chan", scatter_dimension=1, tiled=True
    )


def solution(mesh):
    return jax.shard_map(
        per_device,
        mesh=mesh,
        in_specs=(P("seq", "chan"), P("seq", "chan"), P("seq", "chan"), P("chan"), P("chan", None)),
        out_specs=P("seq", "chan"),
        check_vma=False,
    )
```

profile of v0, /device:TPU:12, one launch (start us, length us, event | category | flops | bytes accessed | tf_op | source)
XLA Modules:
  0.0 498.3 jit_solution(1143848206011449691)
XLA Ops:
  11.6 9.4 %all-to-all-start.3 = ((bf16[32,2,2048]{2,1,0:T(2,128)(2,1)}), bf16[32,2,2048]{2,1,0:T(2,128)(2,1)S(1)}, u32[]{:S(2)}, u32[]{:S(2)}) async-start(bf16[32,2,2048]{2,1,0:T(2,128)(2,1)} %reshape.148), calls=%async_computation.3 | async-start | bytes 524288 | tf_op jit(solution)/shard_map/all_to_all | solution.py:80
  28.5 7.4 %all-to-all-start = ((bf16[32,2,2048]{2,1,0:T(2,128)(2,1)}), bf16[32,2,2048]{2,1,0:T(2,128)(2,1)S(1)}, u32[]{:S(2)}, u32[]{:S(2)}) async-start(bf16[32,2,2048]{2,1,0:T(2,128)(2,1)} %reshape.146), calls=%async_computation | async-start | bytes 524288 | tf_op jit(solution)/shard_map/all_to_all | solution.py:77
  49.8 7.4 %all-to-all-start.4 = ((bf16[64,16,256]{2,1,0:T(8,128)(2,1)}), bf16[64,16,256]{2,1,0:T(8,128)(2,1)S(1)}, u32[]{:S(2)}, u32[]{:S(2)}) async-start(bf16[64,16,256]{2,1,0:T(8,128)(2,1)} %copy.50), calls=%async_computation.4 | async-start | bytes 1048576 | tf_op jit(solution)/shard_map/all_to_all | solution.py:101
  58.3 12.5 %all-to-all-done.4 = bf16[64,16,256]{2,1,0:T(8,128)(2,1)S(1)} async-done(((bf16[64,16,256]{2,1,0:T(8,128)(2,1)}), bf16[64,16,256]{2,1,0:T(8,128)(2,1)S(1)}, u32[]{:S(2)}, u32[]{:S(2)}) %all-to-all-start.4) | async-done | bytes 524320 | tf_op jit(solution)/shard_map/all_to_all | solution.py:101
  70.8 7.0 %all-to-all-start.5 = ((bf16[64,16,256]{2,1,0:T(8,128)(2,1)}), bf16[64,16,256]{2,1,0:T(8,128)(2,1)S(1)}, u32[]{:S(2)}, u32[]{:S(2)}) async-start(bf16[64,16,256]{2,1,0:T(8,128)(2,1)} %copy.52), calls=%async_computation.5 | async-start | bytes 1048576 | tf_op jit(solution)/shard_map/all_to_all | solution.py:104
  80.0 11.5 %all-to-all-done.5 = bf16[64,16,256]{2,1,0:T(8,128)(2,1)S(1)} async-done(((bf16[64,16,256]{2,1,0:T(8,128)(2,1)}), bf16[64,16,256]{2,1,0:T(8,128)(2,1)S(1)}, u32[]{:S(2)}, u32[]{:S(2)}) %all-to-all-start.5) | async-done | bytes 524320 | tf_op jit(solution)/shard_map/all_to_all | solution.py:104
  91.5 7.6 %all-to-all-start.1 = ((bf16[64,16,256]{2,1,0:T(8,128)(2,1)}), bf16[64,16,256]{2,1,0:T(8,128)(2,1)}, u32[]{:S(2)}, u32[]{:S(2)}) async-start(bf16[64,16,256]{2,1,0:T(8,128)(2,1)} %copy.43), calls=%async_computation.1 | async-start | bytes 1048576 | tf_op jit(solution)/shard_map/all_to_all | solution.py:95
  103.1 9.7 %all-to-all-done.1 = bf16[64,16,256]{2,1,0:T(8,128)(2,1)} async-done(((bf16[64,16,256]{2,1,0:T(8,128)(2,1)}), bf16[64,16,256]{2,1,0:T(8,128)(2,1)}, u32[]{:S(2)}, u32[]{:S(2)}) %all-to-all-start.1) | async-done | bytes 524320 | tf_op jit(solution)/shard_map/all_to_all | solution.py:95
  112.8 7.3 %all-to-all-start.2 = ((bf16[64,16,256]{2,1,0:T(8,128)(2,1)}), bf16[64,16,256]{2,1,0:T(8,128)(2,1)S(1)}, u32[]{:S(2)}, u32[]{:S(2)}) async-start(bf16[64,16,256]{2,1,0:T(8,128)(2,1)} %copy.45), calls=%async_computation.2 | async-start | bytes 1048576 | tf_op jit(solution)/shard_map/all_to_all | solution.py:98
  125.9 6.1 %fusion.31 = f32[512,2,256]{2,0,1:T(8,128)} fusion(bf16[2,512,256]{2,1,0:T(8,128)(2,1)S(1)} %bitcast.134), kind=kOutput, calls=%fused_computation.42 | convolution fusion | flops 1614282752 | bytes 1572864 | tf_op jit(solution)/shard_map/krc,rm->kmc/dot_general | solution.py:28
  132.0 6.1 %fusion.25 = f32[512,2,256]{2,0,1:T(8,128)} fusion(bf16[2,512,256]{2,1,0:T(8,128)(2,1)S(1)} %bitcast.136), kind=kOutput, calls=%fused_computation.36 | convolution fusion | flops 1614282752 | bytes 1572864 | tf_op jit(solution)/shard_map/krc,rm->kmc/dot_general | solution.py:28
  138.1 6.5 %fusion.4 = f32[512,2,256]{2,0,1:T(8,128)} fusion(f32[512,2,256]{2,0,1:T(8,128)S(1)} %fusion.29, bf16[2,512,256]{2,1,0:T(8,128)(2,1)S(1)} %bitcast.137), kind=kOutput, calls=%fused_computation.13 | convolution fusion | flops 1614807040 | bytes 2621440 | tf_op jit(solution)/shard_map/krc,rm->kmc/dot_general | solution.py:28
  154.3 4.9 fusion.2
  159.2 5.1 %multiply_subtract_fusion = (f32[512,2,256]{2,0,1:T(8,128)S(1)}, f32[512,2,256]{2,0,1:T(8,128)S(1)}) fusion(f32[512,2,256]{2,0,1:T(8,128)S(1)} %fusion.2, f32[512,2,256]{2,0,1:T(8,128)S(1)} %fusion.5, f32[512,2,256]{2,0,1:T(8,128)S(1)} %copy-done.11, f32[512,2,256]{2,0,1:T(8,128)S(1)} %fusion.27, bf16[2,512,256]{2,1,0:T(8,128)(2,1)S(1)} %bitcast.135), kind=kOutput, calls=%fused_computation.47 | convolution fusion | flops 1616379904 | bytes 6815744 | tf_op jit(solution)/shard_map/krc,rm->kmc/dot_general | solution.py:28
  164.3 5.9 %fusion.11 = f32[512,2,256]{2,0,1:T(8,128)S(1)} fusion(f32[512,2,256]{2,0,1:T(8,128)S(1)} %get-tuple-element.6), kind=kOutput, calls=%fused_computation.22 | convolution fusion | flops 1614282752 | bytes 2097152 | tf_op jit(solution)/shard_map/kmc,mr->krc/dot_general | solution.py:28
  170.2 5.7 %fusion.15 = f32[512,2,256]{2,0,1:T(8,128)S(1)} fusion(f32[512,2,256]{2,0,1:T(8,128)S(1)} %get-tuple-element.5), kind=kOutput, calls=%fused_computation.26 | convolution fusion | flops 1614282752 | bytes 2097152 | tf_op jit(solution)/shard_map/kmc,mr->krc/dot_general | solution.py:28
  175.9 6.0 %fusion = f32[2,512,256]{2,1,0:T(8,128)S(1)} fusion(f32[512,2,256]{2,0,1:T(8,128)S(1)} %fusion.11, f32[512,2,256]{2,0,1:T(8,128)S(1)} %get-tuple-element.5), kind=kOutput, calls=%fused_computation.5 | convolution fusion | flops 1614544896 | bytes 3145728 | tf_op jit(solution)/shard_map/kmc,mr->krc/dot_general | solution.py:28
  181.9 6.4 %add_convert_fusion = (bf16[2,512,256]{2,1,0:T(8,128)(2,1)S(1)}, bf16[2,512,256]{2,1,0:T(8,128)(2,1)S(1)}) fusion(f32[2,512,256]{2,1,0:T(8,128)S(1)} %fusion, f32[2,512]{1,0:T(2,128)S(1)} %get-tuple-element.16, f32[2,512]{1,0:T(2,128)S(1)} %get-tuple-element.15, f32[512,2,256]{2,0,1:T(8,128)S(1)} %fusion.15, f32[512,2,256]{2,0,1:T(8,128)S(1)} %get-tuple-element.6), kind=kOutput, calls=%fused_computation.44 | convolution fusion | flops 1616642048 | bytes 4202496 | tf_op jit(solution)/shard_map/kmc,mr->krc/dot_general | solution.py:28
  189.7 7.7 %all-to-all-start.6 = ((bf16[2,512,256]{2,0,1:T(2,128)(2,1)}), bf16[2,512,256]{2,0,1:T(2,128)(2,1)S(1)}, u32[]{:S(2)}, u32[]{:S(2)}) async-start(bf16[2,512,256]{2,0,1:T(2,128)(2,1)} %copy.54), calls=%async_computation.6 | async-start | bytes 1048576 | tf_op jit(solution)/shard_map/all_to_all | solution.py:117
  198.7 12.3 %all-to-all-done.6 = bf16[2,512,256]{2,0,1:T(2,128)(2,1)S(1)} async-done(((bf16[2,512,256]{2,0,1:T(2,128)(2,1)}), bf16[2,512,256]{2,0,1:T(2,128)(2,1)S(1)}, u32[]{:S(2)}, u32[]{:S(2)}) %all-to-all-start.6) | async-done | bytes 524320 | tf_op jit(solution)/shard_map/all_to_all | solution.py:117
  211.0 7.0 %all-to-all-start.7 = ((bf16[2,512,256]{2,0,1:T(2,128)(2,1)}), bf16[2,512,256]{2,0,1:T(2,128)(2,1)S(1)}, u32[]{:S(2)}, u32[]{:S(2)}) async-start(bf16[2,512,256]{2,0,1:T(2,128)(2,1)} %copy.56), calls=%async_computation.7 | async-start | bytes 1048576 | tf_op jit(solution)/shard_map/all_to_all | solution.py:120
  222.9 8.7 %all-to-all-done.7 = bf16[2,512,256]{2,0,1:T(2,128)(2,1)S(1)} async-done(((bf16[2,512,256]{2,0,1:T(2,128)(2,1)}), bf16[2,512,256]{2,0,1:T(2,128)(2,1)S(1)}, u32[]{:S(2)}, u32[]{:S(2)}) %all-to-all-start.7) | async-done | bytes 524320 | tf_op jit(solution)/shard_map/all_to_all | solution.py:120
  234.8 14.2 %all_to_all.141 = bf16[32,16,256]{2,1,0:T(8,128)(2,1)S(1)} all-to-all(bf16[32,16,256]{2,1,0:T(8,128)(2,1)S(1)} %copy.58), channel_id=1, replica_groups=mesh['seq'=32,'chan'=16] {'seq'}, dimensions={0} | all-to-all | bytes 524288 | tf_op jit(solution)/shard_map/all_to_all | solution.py:128
  252.3 238.8 %reduce-scatter.2.cloned.1.call-done = bf16[512,256]{1,0:T(8,128)(2,1)} async-done(((bf16[512,4096]{1,0:T(8,128)(2,1)}), bf16[512,256]{1,0:T(8,128)(2,1)}) %reduce-scatter.2.cloned.1.call-update) | async-done | bytes 262160 | tf_op jit(solution)/shard_map/reduce_scatter | solution.py:136
  (73 shorter events, 62.9 us)
Async XLA Ops:
  6.5 242.5 %copy-start = (bf16[256,4096]{1,0:T(8,128)(2,1)S(1)}, bf16[256,4096]{1,0:T(8,128)(2,1)}, u32[]{:S(2)}) copy-start(bf16[256,4096]{1,0:T(8,128)(2,1)} %param.9) | copy-start | bytes 6291460
  6.5 14.4 %copy-start.3 = (bf16[512,256]{1,0:T(8,128)(2,1)S(1)}, bf16[512,256]{1,0:T(8,128)(2,1)}, u32[]{:S(2)}) copy-start(bf16[512,256]{1,0:T(8,128)(2,1)} %param.5) | copy-start | bytes 786436
  11.6 17.0 %all-to-all-start.3 = ((bf16[32,2,2048]{2,1,0:T(2,128)(2,1)}), bf16[32,2,2048]{2,1,0:T(2,128)(2,1)S(1)}, u32[]{:S(2)}, u32[]{:S(2)}) async-start(bf16[32,2,2048]{2,1,0:T(2,128)(2,1)} %reshape.148), calls=%async_computation.3 | async-start | bytes 524288 | tf_op jit(solution)/shard_map/all_to_all | solution.py:80
  28.5 15.0 %all-to-all-start = ((bf16[32,2,2048]{2,1,0:T(2,128)(2,1)}), bf16[32,2,2048]{2,1,0:T(2,128)(2,1)S(1)}, u32[]{:S(2)}, u32[]{:S(2)}) async-start(bf16[32,2,2048]{2,1,0:T(2,128)(2,1)} %reshape.146), calls=%async_computation | async-start | bytes 524288 | tf_op jit(solution)/shard_map/all_to_all | solution.py:77
  44.5 1.9 copy-start.1
  48.7 8.5 %copy-start.2 = (bf16[64,16,256]{2,0,1:T(8,128)(2,1)S(1)}, bf16[64,16,256]{2,0,1:T(8,128)(2,1)}, u32[]{:S(2)}) copy-start(bf16[64,16,256]{2,0,1:T(8,128)(2,1)} %get-tuple-element.14) | copy-start | bytes 1572868
  49.8 21.1 %all-to-all-start.4 = ((bf16[64,16,256]{2,1,0:T(8,128)(2,1)}), bf16[64,16,256]{2,1,0:T(8,128)(2,1)S(1)}, u32[]{:S(2)}, u32[]{:S(2)}) async-start(bf16[64,16,256]{2,1,0:T(8,128)(2,1)} %copy.50), calls=%async_computation.4 | async-start | bytes 1048576 | tf_op jit(solution)/shard_map/all_to_all | solution.py:101
  70.8 20.6 %all-to-all-start.5 = ((bf16[64,16,256]{2,1,0:T(8,128)(2,1)}), bf16[64,16,256]{2,1,0:T(8,128)(2,1)S(1)}, u32[]{:S(2)}, u32[]{:S(2)}) async-start(bf16[64,16,256]{2,1,0:T(8,128)(2,1)} %copy.52), calls=%async_computation.5 | async-start | bytes 1048576 | tf_op jit(solution)/shard_map/all_to_all | solution.py:104
  91.5 21.3 %all-to-all-start.1 = ((bf16[64,16,256]{2,1,0:T(8,128)(2,1)}), bf16[64,16,256]{2,1,0:T(8,128)(2,1)}, u32[]{:S(2)}, u32[]{:S(2)}) async-start(bf16[64,16,256]{2,1,0:T(8,128)(2,1)} %copy.43), calls=%async_computation.1 | async-start | bytes 1048576 | tf_op jit(solution)/shard_map/all_to_all | solution.py:95
  103.1 18.1 %copy-start.5 = (bf16[32,2,16,256]{3,2,0,1:T(8,128)(2,1)S(1)}, bf16[32,2,16,256]{3,2,0,1:T(8,128)(2,1)}, u32[]{:S(2)}) copy-start(bf16[32,2,16,256]{3,2,0,1:T(8,128)(2,1)} %copy.51) | copy-start | bytes 1572868
  112.8 31.8 %all-to-all-start.2 = ((bf16[64,16,256]{2,1,0:T(8,128)(2,1)}), bf16[64,16,256]{2,1,0:T(8,128)(2,1)S(1)}, u32[]{:S(2)}, u32[]{:S(2)}) async-start(bf16[64,16,256]{2,1,0:T(8,128)(2,1)} %copy.45), calls=%async_computation.2 | async-start | bytes 1048576 | tf_op jit(solution)/shard_map/all_to_all | solution.py:98
  121.2 4.8 copy-start.6
  125.9 6.1 %copy-start.8 = (bf16[32,2,16,256]{3,2,0,1:T(8,128)(2,1)S(1)}, bf16[32,2,16,256]{3,2,0,1:T(8,128)(2,1)}, u32[]{:S(2)}) copy-start(bf16[32,2,16,256]{3,2,0,1:T(8,128)(2,1)} %copy.53) | copy-start | bytes 1572868
  144.7 4.8 copy-start.13
  149.4 4.8 copy-start.12
  154.3 5.0 copy-start.7
  154.3 5.0 copy-start.11
  189.7 21.3 %all-to-all-start.6 = ((bf16[2,512,256]{2,0,1:T(2,128)(2,1)}), bf16[2,512,256]{2,0,1:T(2,128)(2,1)S(1)}, u32[]{:S(2)}, u32[]{:S(2)}) async-start(bf16[2,512,256]{2,0,1:T(2,128)(2,1)} %copy.54), calls=%async_computation.6 | async-start | bytes 1048576 | tf_op jit(solution)/shard_map/all_to_all | solution.py:117
  211.0 20.6 %all-to-all-start.7 = ((bf16[2,512,256]{2,0,1:T(2,128)(2,1)}), bf16[2,512,256]{2,0,1:T(2,128)(2,1)S(1)}, u32[]{:S(2)}, u32[]{:S(2)}) async-start(bf16[2,512,256]{2,0,1:T(2,128)(2,1)} %copy.56), calls=%async_computation.7 | async-start | bytes 1048576 | tf_op jit(solution)/shard_map/all_to_all | solution.py:120
  218.0 273.1 %reduce-scatter.2.cloned.1.call-start = ((), (), s32[]{:S(2)}) async-start(), calls=%async_computation.10 | async-start | bytes 4456448 | tf_op jit(solution)/shard_map/reduce_scatter | solution.py:136
  231.6 17.4 %copy-start.4 = (bf16[512,256]{1,0:T(8,128)(2,1)S(1)}, bf16[512,256]{1,0:T(8,128)(2,1)}, u32[]{:S(2)}) copy-start(bf16[512,256]{1,0:T(8,128)(2,1)} %param.5) | copy-start | bytes 786436
  231.6 17.4 %copy-start.10 = (f32[256]{0:T(256)S(1)}, f32[256]{0:T(256)}, u32[]{:S(2)}) copy-start(f32[256]{0:T(256)} %param.8) | copy-start | bytes 3076
  234.2 14.9 %copy-start.9 = (bf16[512,256]{1,0:T(8,128)(2,1)S(1)}, bf16[512,256]{1,0:T(8,128)(2,1)}, u32[]{:S(2)}) copy-start(bf16[512,256]{1,0:T(8,128)(2,1)} %param.6) | copy-start | bytes 786436
Sparse Core Ops, SparseCore 0:
  252.4 238.5 reduce-scatter.1
where the time goes:
time: 508 us; the launch traced here: 498 us
  waiting for transfers between devices  302 us (59%)
  matrix products  77.4 us (15%)
  starting transfers between devices  60.8 us (12%)
  local copies, waits for them, and re-layouts  24.5 us (5%)
  between operations  14.3 us (3%)
  blocking collectives  14.2 us (3%)
    reduce_scatter x1, waiting for transfers between devices, per_device(): lax.psum_scatter(partial_sums.astype(jnp.bfloat16), 'chan', scatter_dimen...  239 us
    dot_general x16, matrix products, contract(): return jnp.einsum(form, values, table, precision=HIGH)  72.3 us
    all_to_all x1, blocking collectives, per_device(): lax.all_to_all(as_sent(rows_values), 'seq', split_axis=0, concat_axis=1,...  14.2 us
    all_to_all x1, waiting for transfers between devices, per_device(): lax.all_to_all(ker_real.astype(jnp.bfloat16), 'seq', split_axis=0, concat...  12.5 us
    all_to_all x1, waiting for transfers between devices, per_device(): lax.all_to_all(as_sent(back_real), 'seq', split_axis=1, concat_axis=0, ti...  12.3 us
    all_to_all x1, waiting for transfers between devices, per_device(): lax.all_to_all(ker_imag.astype(jnp.bfloat16), 'seq', split_axis=0, concat...  11.5 us
  transfers between devices with their start and end apart: 9, of which 8 were waited for; matrix products, arithmetic and copies ran while one was open for 8% of the time, Pallas kernels for 0%

commit v1 on v0

v1 whole, which is shorter than its diff:
```python
import functools

import jax
import jax.numpy as jnp
import ml_dtypes
import numpy as np
from jax import lax
from jax.experimental import pallas as pl
from jax.experimental.pallas import tpu as pltpu
from jax.sharding import PartitionSpec as P

MESH = pl.DeviceIdType.MESH
F32 = jnp.float32
BF16 = jnp.bfloat16
SEQ = 32
Z = 8
LANES = 128
TOK = 512
CH = 256
SEGS = TOK // LANES
HALVES = 2
CHUNK_CH = CH // HALVES
OWN = CHUNK_CH // SEQ
ROWS = OWN * SEGS
TOK_CHUNKS = 4
PIECE = TOK // TOK_CHUNKS
SHARE = 32
SHARES = CH // SHARE


def tables():
    freq = (2 * np.arange(128) + 1) * np.pi / 256
    angle = np.arange(256)[:, None] * freq[None, :]
    both = np.concatenate([np.cos(angle), np.sin(angle)], axis=1)
    to_lane = both[:128]
    to_row = both[:128].T
    from_row = both[:128]
    from_lane = both.T
    return tuple(t.astype(ml_dtypes.bfloat16) for t in (to_lane, to_row, from_row, from_lane))


def dot(left, right):
    return jnp.dot(left, right, preferred_element_type=F32)


def spectrum_product(left, right):
    lcc, lcs, lsc, lss = left[:128, :128], left[:128, 128:], left[128:, :128], left[128:, 128:]
    rcc, rcs, rsc, rss = right[:128, :128], right[:128, 128:], right[128:, :128], right[128:, 128:]
    cc = lcc * rcc - lcs * rcs - lsc * rsc + lss * rss
    cs = lcc * rcs + lcs * rcc - lsc * rss - lss * rsc
    sc = lcc * rsc - lcs * rss + lsc * rcc - lss * rcs
    ss = lcc * rss + lcs * rsc + lsc * rcs + lss * rcc
    top = jnp.concatenate([cc, cs], axis=1)
    bottom = jnp.concatenate([sc, ss], axis=1)
    return jnp.concatenate([top, bottom], axis=0).astype(BF16)


def kernel(
    kv_ref, gate_ref, filt_ref, skip_ref, w_ref, to_lane, to_row, from_row, from_lane,
    out_ref,
    spread, send_a, recv_a, rows_x, rows_h, rows_y, send_c, recv_c, rows_c,
    gated, weights, acc, part_out, part_in,
    a_send, a_recv, c_send, c_recv, w1_send, w1_recv, w2_send, w2_recv, w3_send, w3_recv, w_local,
    right_send, right_recv, left_send, left_recv, y_send, y_recv,
):
    me = lax.axis_index("seq")
    chan = lax.axis_index("chan")
    y_hi = chan // Z
    z = lax.rem(chan, Z)
    core = lax.rem(me, 2)
    x = me // 8
    share = x * 2 + core

    def chan_of(hi, zz):
        return hi * Z + lax.rem(zz, Z)

    right, left = chan_of(y_hi, z + 1), chan_of(y_hi, z + Z - 1)
    partner = chan_of(1 - y_hi, z)
    barrier = pltpu.get_barrier_semaphore()

    def greet_seq(k, carry):
        pl.semaphore_signal(
            barrier, inc=1, device_id={"seq": lax.rem(me + k, SEQ)}, device_id_type=MESH
        )
        return carry

    def greet_z(k, carry):
        pl.semaphore_signal(
            barrier, inc=1, device_id={"chan": chan_of(y_hi, z + k)}, device_id_type=MESH
        )
        return carry

    lax.fori_loop(1, SEQ, greet_seq, 0)
    lax.fori_loop(1, Z, greet_z, 0)
    pl.semaphore_signal(barrier, inc=1, device_id={"chan": partner}, device_id_type=MESH)

    for which, source in enumerate((kv_ref, filt_ref)):
        for seg in range(SEGS):
            for part in range(CH // LANES):
                block = source[seg * LANES : (seg + 1) * LANES, part * LANES : (part + 1) * LANES]
                turned = block.astype(F32).T
                for quarter in range(LANES // SEQ):
                    index = part * (LANES // SEQ) + quarter
                    half, own = index // OWN, index % OWN
                    spread[half, pl.ds(seg * OWN + own, SEQ, stride=ROWS), :] = turned[
                        quarter * SEQ : (quarter + 1) * SEQ
                    ]
        for half in range(HALVES):
            send_a[half, :, which * ROWS : (which + 1) * ROWS, :] = (
                spread[half].reshape(SEQ, ROWS, LANES).astype(BF16)
            )
    for half in range(HALVES):
        recv_a[half, me] = send_a[half, me]

    own_copies = [
        pltpu.make_async_copy(
            w_ref.at[
                pl.ds(pl.multiple_of(share * SHARE, SHARE), SHARE),
                pl.ds(
                    pl.multiple_of((y_hi + rel - 2 * y_hi * rel) * Z * CH + z * CH, CH), CH
                ),
            ],
            weights.at[share, z, rel],
            w_local.at[rel],
        )
        for rel in range(2)
    ]
    for copy in own_copies:
        copy.start()

    pl.semaphore_wait(barrier, SEQ - 1 + Z - 1 + 1)

    def send_signal(half):
        def one(k, carry):
            peer = lax.rem(me + k, SEQ)
            pltpu.make_async_remote_copy(
                src_ref=send_a.at[half, peer],
                dst_ref=recv_a.at[half, me],
                send_sem=a_send.at[half],
                recv_sem=a_recv.at[half],
                device_id={"seq": peer},
                device_id_type=MESH,
            ).start()
            return carry

        lax.fori_loop(1, SEQ, one, 0)

    def wait_bytes(ref, sem):
        pltpu.make_async_copy(ref, ref, sem).wait()

    for half in range(HALVES):
        send_signal(half)

    def send_weight(k, carry):
        to = lax.rem(z + k, Z)
        for rel in range(2):
            column = (y_hi + rel - 2 * y_hi * rel) * Z * CH + to * CH
            pltpu.make_async_remote_copy(
                src_ref=w_ref.at[
                    pl.ds(pl.multiple_of(share * SHARE, SHARE), SHARE),
                    pl.ds(pl.multiple_of(column, CH), CH),
                ],
                dst_ref=weights.at[share, z, rel],
                send_sem=w1_send,
                recv_sem=w1_recv,
                device_id={"chan": chan_of(y_hi, to)},
                device_id_type=MESH,
            ).start()
        return carry

    lax.fori_loop(1, Z, send_weight, 0)

    def convolve(half):
        rows_x[...] = recv_a[half, :, :ROWS, :].astype(F32).reshape(SEQ * ROWS, LANES)
        rows_h[...] = recv_a[half, :, ROWS:, :].astype(F32).reshape(SEQ * ROWS, LANES)
        first_row = lax.broadcasted_iota(jnp.int32, (LANES, LANES), 0) == 0
        for own in range(OWN):
            spectra = []
            for rows in (rows_x, rows_h):
                blocks = rows[pl.ds(own, LANES, stride=OWN), :].astype(BF16)
                lane_freq = dot(blocks, to_lane[...]).astype(BF16)
                spectra.append(dot(to_row[...], lane_freq))
            product = spectrum_product(*spectra)
            back = dot(from_row[...], product).astype(BF16)
            wide = dot(back, from_lane[...])
            carried = jnp.where(first_row, 0.0, pltpu.roll(wide[:, LANES:], 1, 0))
            rows_y[pl.ds(own, LANES, stride=OWN), :] = (wide[:, :LANES] + carried) * (
                1.0 / (128 * 128)
            )
        send_c[half] = rows_y[...].reshape(SEQ, ROWS, LANES).astype(BF16)
        recv_c[half, me] = send_c[half, me]

    def send_back(half):
        def one(k, carry):
            peer = lax.rem(me + k, SEQ)
            pltpu.make_async_remote_copy(
                src_ref=send_c.at[half, peer],
                dst_ref=recv_c.at[half, me],
                send_sem=c_send.at[half],
                recv_sem=c_recv.at[half],
                device_id={"seq": peer},
                device_id_type=MESH,
            ).start()
            return carry

        lax.fori_loop(1, SEQ, one, 0)

    others = pl.ds(0, SEQ - 1)

    def second_leg(k, carry):
        peer = lax.rem(me + 8 * k, SEQ)
        pltpu.make_async_remote_copy(
            src_ref=weights.at[share],
            dst_ref=weights.at[share],
            send_sem=w2_send,
            recv_sem=w2_recv,
            device_id={"seq": peer},
            device_id_type=MESH,
        ).start()
        return carry

    def third_leg(k, carry):
        which = 2 * k + core
        pltpu.make_async_remote_copy(
            src_ref=weights.at[which],
            dst_ref=weights.at[which],
            send_sem=w3_send,
            recv_sem=w3_recv,
            device_id={"seq": me + 1 - 2 * core},
            device_id_type=MESH,
        ).start()
        return carry

    seven = weights.at[0, pl.ds(0, Z - 1)]
    for half in range(HALVES):
        wait_bytes(recv_a.at[half, others], a_recv.at[half])
        convolve(half)
        send_back(half)
        if half == 0:
            for copy in own_copies:
                copy.wait()
            wait_bytes(seven, w1_recv)
            lax.fori_loop(1, 4, second_leg, 0)
    wait_bytes(weights.at[pl.ds(0, 3)], w2_recv)
    lax.fori_loop(0, 4, third_leg, 0)

    def piece(block, half, chunk):
        return gated.at[block, half, pl.ds(chunk * PIECE, PIECE)]

    def to_right(half, step, chunk):
        ref = piece(lax.rem(z - step + Z, Z), half, chunk)
        return pltpu.make_async_remote_copy(
            src_ref=ref,
            dst_ref=ref,
            send_sem=right_send.at[half, step, chunk],
            recv_sem=right_recv.at[half, step, chunk],
            device_id={"chan": right},
            device_id_type=MESH,
        )

    def to_left(half, step, chunk):
        ref = piece(lax.rem(z + step, Z), half, chunk)
        return pltpu.make_async_remote_copy(
            src_ref=ref,
            dst_ref=ref,
            send_sem=left_send.at[half, step, chunk],
            recv_sem=left_recv.at[half, step, chunk],
            device_id={"chan": left},
            device_id_type=MESH,
        )

    def arrive(ref, sem):
        pltpu.make_async_copy(ref, ref, sem).wait()

    def goes_right(step, chunk):
        return step < 3 or (step == 3 and chunk < TOK_CHUNKS // 2)

    def goes_left(step, chunk):
        return step < 3 or (step == 3 and chunk >= TOK_CHUNKS // 2)

    def add_block(block, half, first):
        shares = CHUNK_CH // SHARE
        for rel in range(2):
            weight = weights[half * shares : (half + 1) * shares, block, rel].reshape(CHUNK_CH, CH)
            term = dot(gated[block, half], weight)
            if first:
                acc[rel] = term
            else:
                acc[rel] += term

    for half in range(HALVES):
        wait_bytes(recv_c.at[half, others], c_recv.at[half])
        rows_c[...] = recv_c[half].astype(F32).reshape(SEQ * ROWS, LANES)
        for seg in range(SEGS):
            columns = []
            for part in range(CHUNK_CH // LANES):
                per = LANES // SEQ
                stacked = jnp.concatenate(
                    [
                        rows_c[pl.ds(seg * OWN + part * per + own, SEQ, stride=ROWS), :]
                        for own in range(per)
                    ],
                    axis=0,
                )
                columns.append(stacked.T)
            conv = jnp.concatenate(columns, axis=1) if len(columns) > 1 else columns[0]
            tokens = slice(seg * LANES, (seg + 1) * LANES)
            chans = slice(half * CHUNK_CH, (half + 1) * CHUNK_CH)
            signal = kv_ref[tokens, chans].astype(F32)
            value = gate_ref[tokens, chans].astype(F32) * (conv + skip_ref[:, chans] * signal)
            gated[z, half, tokens, :] = value.astype(BF16)
        for chunk in range(TOK_CHUNKS):
            to_right(half, 0, chunk).start()
            to_left(half, 0, chunk).start()

    wait_bytes(weights.at[pl.ds(0, 4)], w3_recv)

    for half in range(HALVES):
        add_block(z, half, half == 0)
        for step in range(4):
            from_left = lax.rem(z + Z - step - 1, Z)
            from_right = lax.rem(z + step + 1, Z)
            for chunk in range(TOK_CHUNKS):
                if goes_right(step, chunk):
                    arrive(piece(from_left, half, chunk), right_recv.at[half, step, chunk])
                    if goes_right(step + 1, chunk):
                        to_right(half, step + 1, chunk).start()
                if goes_left(step, chunk):
                    arrive(piece(from_right, half, chunk), left_recv.at[half, step, chunk])
                    if goes_left(step + 1, chunk):
                        to_left(half, step + 1, chunk).start()
            add_block(from_left, half, False)
            if step < 3:
                add_block(from_right, half, False)

    part_out[...] = acc[1].astype(BF16)
    exchange = pltpu.make_async_remote_copy(
        src_ref=part_out,
        dst_ref=part_in,
        send_sem=y_send,
        recv_sem=y_recv,
        device_id={"chan": partner},
        device_id_type=MESH,
    )
    exchange.start()

    for half in range(HALVES):
        wait_bytes(send_a.at[half, others], a_send.at[half])
        wait_bytes(send_c.at[half, others], c_send.at[half])
        for step in range(4):
            for chunk in range(TOK_CHUNKS):
                if goes_right(step, chunk):
                    arrive(piece(0, half, chunk), right_send.at[half, step, chunk])
                if goes_left(step, chunk):
                    arrive(piece(0, half, chunk), left_send.at[half, step, chunk])
    wait_bytes(seven, w1_send)
    wait_bytes(weights.at[pl.ds(0, 3)], w2_send)
    wait_bytes(weights.at[pl.ds(0, 4)], w3_send)
    exchange.wait()
    out_ref[...] = (acc[0] + part_in[...].astype(F32)).astype(BF16)


def per_device(key_value, gating, long_filter, skip_gain, out_weight):
    vmem = pl.BlockSpec(memory_space=pltpu.VMEM)
    anywhere = pl.BlockSpec(memory_space=pl.ANY)
    dma = pltpu.SemaphoreType.DMA
    ring = dma((HALVES, 4, TOK_CHUNKS))
    return pl.pallas_call(
        kernel,
        out_shape=jax.ShapeDtypeStruct((TOK, CH), BF16),
        in_specs=[vmem, vmem, vmem, vmem, anywhere, vmem, vmem, vmem, vmem],
        out_specs=vmem,
        scratch_shapes=[
            pltpu.VMEM((HALVES, SEQ * ROWS, LANES), F32),
            pltpu.VMEM((HALVES, SEQ, 2 * ROWS, LANES), BF16),
            pltpu.VMEM((HALVES, SEQ, 2 * ROWS, LANES), BF16),
            pltpu.VMEM((SEQ * ROWS, LANES), F32),
            pltpu.VMEM((SEQ * ROWS, LANES), F32),
            pltpu.VMEM((SEQ * ROWS, LANES), F32),
            pltpu.VMEM((HALVES, SEQ, ROWS, LANES), BF16),
            pltpu.VMEM((HALVES, SEQ, ROWS, LANES), BF16),
            pltpu.VMEM((SEQ * ROWS, LANES), F32),
            pltpu.VMEM((Z, HALVES, TOK, CHUNK_CH), BF16),
            pltpu.VMEM((SHARES, Z, 2, SHARE, CH), BF16),
            pltpu.VMEM((2, TOK, CH), F32),
            pltpu.VMEM((TOK, CH), BF16),
            pltpu.VMEM((TOK, CH), BF16),
            dma((HALVES,)), dma((HALVES,)), dma((HALVES,)), dma((HALVES,)),
            dma, dma, dma, dma, dma, dma, dma((2,)),
            ring, ring, ring, ring,
            dma, dma,
        ],
        compiler_params=pltpu.CompilerParams(
            collective_id=0, has_side_effects=True, vmem_limit_bytes=48 * 2**20
        ),
    )(
        key_value, gating, long_filter, skip_gain.reshape(1, CH), out_weight,
        *(jnp.asarray(t) for t in tables()),
    )


def solution(mesh):
    return jax.shard_map(
        per_device,
        mesh=mesh,
        in_specs=(P("seq", "chan"), P("seq", "chan"), P("seq", "chan"), P("chan"), P("chan", None)),
        out_specs=P("seq", "chan"),
        check_vma=False,
    )
```

time: 508 us -> 95.3 us (0.19)
  the two profiles are of different devices: /device:TPU:12 before, /device:TPU:8 now
where the time goes in v1:
time: 95.3 us; the launch traced here: 95 us
  Pallas kernels  86.5 us (91%)
  local copies, waits for them, and re-layouts  8.4 us (9%)
    pallas_call x1, Pallas kernels, per_device(): pl.pallas_call(kernel, out_shape=jax.ShapeDtypeStruct((TOK, CH), BF16), i...  86.5 us
    unnamed x17, local copies, waits for them, and re-layouts  8.4 us

profile of v1, /device:TPU:8, one launch (start us, length us, event | category | flops | bytes accessed | tf_op | source)
XLA Modules:
  0.0 95.0 jit_solution(6023503186539328949)
XLA Ops:
  0.0 0.0 copy-start
  0.0 1.6 %copy-done = bf16[256,4096]{1,0:T(8,128)(2,1)S(1)} copy-done((bf16[256,4096]{1,0:T(8,128)(2,1)S(1)}, bf16[256,4096]{1,0:T(8,128)(2,1)}, u32[]{:S(2)}) %copy-start) | copy-done | bytes 2097176
  1.6 0.0 copy-start.1
  1.6 0.9 copy-done.1
  2.5 0.0 copy-start.2
  2.5 0.9 copy-done.2
  3.5 0.0 copy-start.3
  3.5 0.9 copy-done.3
  4.4 0.0 copy-start.4
  4.4 0.8 copy-done.4
  5.3 0.0 copy-start.5
  5.3 0.9 copy-done.5
  6.2 0.0 copy-start.6
  6.2 0.8 copy-done.6
  7.0 0.0 copy-start.7
  7.0 0.7 copy-done.7
  7.7 86.5 %shard_map.91 = bf16[512,256]{1,0:T(8,128)(2,1)S(1)} custom-call(bf16[512,256]{1,0:T(8,128)(2,1)S(1)} %copy-done.1, bf16[512,256]{1,0:T(8,128)(2,1)S(1)} %copy-done.2, bf16[512,256]{1,0:T(8,128)(2,1)S(1)} %copy-done.3, f32[1,256]{1,0:T(1,128)S(1)} %bitcast.1, bf16[256,4096]{1,0:T(8,128)(2,1)S(1)} %copy-done, bf16[128,256]{1,0:T(8,128)(2,1)S(1)} %copy-done.4, ...), custom_call_target="tpu_custom_call" | custom-call | tf_op jit(solution)/shard_map/pallas_call | solution.py:368
  94.3 0.7 copy.11
Async XLA Ops:
  0.0 1.6 %copy-start = (bf16[256,4096]{1,0:T(8,128)(2,1)S(1)}, bf16[256,4096]{1,0:T(8,128)(2,1)}, u32[]{:S(2)}) copy-start(bf16[256,4096]{1,0:T(8,128)(2,1)} %w_ref.1) | copy-start | bytes 6291460
  1.6 0.9 %copy-start.1 = (bf16[512,256]{1,0:T(8,128)(2,1)S(1)}, bf16[512,256]{1,0:T(8,128)(2,1)}, u32[]{:S(2)}) copy-start(bf16[512,256]{1,0:T(8,128)(2,1)} %kv_ref.1) | copy-start | bytes 786436
  2.5 0.9 %copy-start.2 = (bf16[512,256]{1,0:T(8,128)(2,1)S(1)}, bf16[512,256]{1,0:T(8,128)(2,1)}, u32[]{:S(2)}) copy-start(bf16[512,256]{1,0:T(8,128)(2,1)} %gate_ref.1) | copy-start | bytes 786436
  3.5 0.9 %copy-start.3 = (bf16[512,256]{1,0:T(8,128)(2,1)S(1)}, bf16[512,256]{1,0:T(8,128)(2,1)}, u32[]{:S(2)}) copy-start(bf16[512,256]{1,0:T(8,128)(2,1)} %filt_ref.1) | copy-start | bytes 786436
  4.4 0.8 copy-start.4
  5.3 0.9 copy-start.5
  6.2 0.8 copy-start.6
  7.0 0.7 copy-start.7

commit v2 on v1

--- a/solution.py
+++ b/solution.py
@@ -24,6 +24,12 @@
 ROWS = OWN * SEGS
 TOK_CHUNKS = 4
 PIECE = TOK // TOK_CHUNKS
+GROUPS = 2
+GROUP = TOK // GROUPS
+ORDER = (
+    (0, 0, 1), (0, 1, 1), (1, 0, 0), (0, 0, 2), (0, 1, 2), (1, 0, 1), (1, 1, -1), (0, 0, 3), (0, 1, 3),
+    (1, 0, 2), (1, 1, 0), (1, 0, 3), (1, 1, 1), (1, 1, 2), (1, 1, 3),
+)
 SHARE = 32
 SHARES = CH // SHARE
 
@@ -56,8 +62,9 @@
 
 
 def kernel(
-    kv_ref, gate_ref, filt_ref, skip_ref, w_ref, to_lane, to_row, from_row, from_lane,
+    kv_hbm, gate_hbm, filt_hbm, skip_hbm, w_ref, to_lane_hbm, to_row_hbm, from_row_hbm, from_lane_hbm,
     out_ref,
+    kv_ref, gate_ref, filt_ref, skip_ref, to_lane, to_row, from_row, from_lane, load_sem,
     spread, send_a, recv_a, rows_x, rows_h, rows_y, send_c, recv_c, rows_c,
     gated, weights, acc, part_out, part_in,
     a_send, a_recv, c_send, c_recv, w1_send, w1_recv, w2_send, w2_recv, w3_send, w3_recv, w_local,
@@ -93,6 +100,20 @@
     lax.fori_loop(1, SEQ, greet_seq, 0)
     lax.fori_loop(1, Z, greet_z, 0)
     pl.semaphore_signal(barrier, inc=1, device_id={"chan": partner}, device_id_type=MESH)
+
+    loads = [
+        pltpu.make_async_copy(source, target, load_sem.at[at])
+        for at, (source, target) in enumerate(
+            (
+                (kv_hbm, kv_ref), (filt_hbm, filt_ref), (to_lane_hbm, to_lane), (to_row_hbm, to_row),
+                (from_row_hbm, from_row), (from_lane_hbm, from_lane), (gate_hbm, gate_ref), (skip_hbm, skip_ref),
+            )
+        )
+    ]
+    for load in loads:
+        load.start()
+    loads[0].wait()
+    loads[1].wait()
 
     for which, source in enumerate((kv_ref, filt_ref)):
         for seg in range(SEGS):
@@ -128,6 +149,10 @@
     for copy in own_copies:
         copy.start()
 
+    for load in loads[2:]:
+        load.wait()
+    for copy in own_copies:
+        copy.wait()
     pl.semaphore_wait(barrier, SEQ - 1 + Z - 1 + 1)
 
     def send_signal(half):
@@ -147,9 +172,6 @@
 
     def wait_bytes(ref, sem):
         pltpu.make_async_copy(ref, ref, sem).wait()
-
-    for half in range(HALVES):
-        send_signal(half)
 
     def send_weight(k, carry):
         to = lax.rem(z + k, Z)
@@ -169,6 +191,8 @@
         return carry
 
     lax.fori_loop(1, Z, send_weight, 0)
+    for half in range(HALVES):
+        send_signal(half)
 
     def convolve(half):
         rows_x[...] = recv_a[half, :, :ROWS, :].astype(F32).reshape(SEQ * ROWS, LANES)
@@ -232,17 +256,12 @@
         return carry
 
     seven = weights.at[0, pl.ds(0, Z - 1)]
+    wait_bytes(seven, w1_recv)
+    lax.fori_loop(1, 4, second_leg, 0)
     for half in range(HALVES):
         wait_bytes(recv_a.at[half, others], a_recv.at[half])
         convolve(half)
         send_back(half)
-        if half == 0:
-            for copy in own_copies:
-                copy.wait()
-            wait_bytes(seven, w1_recv)
-            lax.fori_loop(1, 4, second_leg, 0)
-    wait_bytes(weights.at[pl.ds(0, 3)], w2_recv)
-    lax.fori_loop(0, 4, third_leg, 0)
 
     def piece(block, half, chunk):
         return gated.at[block, half, pl.ds(chunk * PIECE, PIECE)]
@@ -273,22 +292,30 @@
         pltpu.make_async_copy(ref, ref, sem).wait()
 
     def goes_right(step, chunk):
-        return step < 3 or (step == 3 and chunk < TOK_CHUNKS // 2)
+        return step < 3 or (step == 3 and chunk % 2 == 0)
 
     def goes_left(step, chunk):
-        return step < 3 or (step == 3 and chunk >= TOK_CHUNKS // 2)
-
-    def add_block(block, half, first):
+        return step < 3 or (step == 3 and chunk % 2 == 1)
+
+    def tokens_of(group):
+        return pl.ds(group * GROUP, GROUP)
+
+    def chunks_of(group):
+        per = TOK_CHUNKS // GROUPS
+        return range(group * per, (group + 1) * per)
+
+    def add_block(block, half, group, first=False):
         shares = CHUNK_CH // SHARE
+        tokens = tokens_of(group)
         for rel in range(2):
             weight = weights[half * shares : (half + 1) * shares, block, rel].reshape(CHUNK_CH, CH)
-            term = dot(gated[block, half], weight)
+            term = dot(gated[block, half, tokens], weight)
             if first:
-                acc[rel] = term
+                acc[rel, tokens] = term
             else:
-                acc[rel] += term
-
-    for half in range(HALVES):
+                acc[rel, tokens] += term
+
+    def gate(half):
         wait_bytes(recv_c.at[half, others], c_recv.at[half])
         rows_c[...] = recv_c[half].astype(F32).reshape(SEQ * ROWS, LANES)
         for seg in range(SEGS):
@@ -309,40 +336,68 @@
             signal = kv_ref[tokens, chans].astype(F32)
             value = gate_ref[tokens, chans].astype(F32) * (conv + skip_ref[:, chans] * signal)
             gated[z, half, tokens, :] = value.astype(BF16)
-        for chunk in range(TOK_CHUNKS):
+
+    def start_group(half, group):
+        for chunk in chunks_of(group):
             to_right(half, 0, chunk).start()
             to_left(half, 0, chunk).start()
 
+    def sources(step):
+        return lax.rem(z + Z - step - 1, Z), lax.rem(z + step + 1, Z)
+
+    def pass_on(half, group, step):
+        from_left, from_right = sources(step)
+        for chunk in chunks_of(group):
+            if goes_right(step, chunk):
+                arrive(piece(from_left, half, chunk), right_recv.at[half, step, chunk])
+                if goes_right(step + 1, chunk):
+                    to_right(half, step + 1, chunk).start()
+            if goes_left(step, chunk):
+                arrive(piece(from_right, half, chunk), left_recv.at[half, step, chunk])
+                if goes_left(step + 1, chunk):
+                    to_left(half, step + 1, chunk).start()
+
+    def add_step(half, group, step):
+        from_left, from_right = sources(step)
+        add_block(from_left, half, group)
+        if step < 3:
+            add_block(from_right, half, group)
+
+    gate(0)
+    for group in range(GROUPS):
+        start_group(0, group)
+    wait_bytes(weights.at[pl.ds(0, 3)], w2_recv)
+    lax.fori_loop(0, 4, third_leg, 0)
+    for group in range(GROUPS):
+        pass_on(0, group, 0)
+    gate(1)
+    start_group(1, 0)
     wait_bytes(weights.at[pl.ds(0, 4)], w3_recv)
-
-    for half in range(HALVES):
-        add_block(z, half, half == 0)
-        for step in range(4):
-            from_left = lax.rem(z + Z - step - 1, Z)
-            from_right = lax.rem(z + step + 1, Z)
-            for chunk in range(TOK_CHUNKS):
-                if goes_right(step, chunk):
-                    arrive(piece(from_left, half, chunk), right_recv.at[half, step, chunk])
-                    if goes_right(step + 1, chunk):
-                        to_right(half, step + 1, chunk).start()
-                if goes_left(step, chunk):
-                    arrive(piece(from_right, half, chunk), left_recv.at[half, step, chunk])
-                    if goes_left(step + 1, chunk):
-                        to_left(half, step + 1, chunk).start()
-            add_block(from_left, half, False)
-            if step < 3:
-                add_block(from_right, half, False)
-
-    part_out[...] = acc[1].astype(BF16)
-    exchange = pltpu.make_async_remote_copy(
-        src_ref=part_out,
-        dst_ref=part_in,
-        send_sem=y_send,
-        recv_sem=y_recv,
-        device_id={"chan": partner},
-        device_id_type=MESH,
-    )
-    exchange.start()
+    for group in range(GROUPS):
+        add_block(z, 0, group, True)
+        add_block(z, 1, group)
+        add_step(0, group, 0)
+
+    exchanges = []
+    for half, group, step in ORDER:
+        if step < 0:
+            start_group(half, group)
+            continue
+        pass_on(half, group, step)
+        add_step(half, group, step)
+        if half == HALVES - 1 and step == 3:
+            tokens = tokens_of(group)
+            part_out[tokens] = acc[1, tokens].astype(BF16)
+            exchange = pltpu.make_async_remote_copy(
+                src_ref=part_out.at[tokens],
+                dst_ref=part_in.at[tokens],
+                send_sem=y_send.at[group],
+                recv_sem=y_recv.at[group],
+                device_id={"chan": partner},
+                device_id_type=MESH,
+            )
+            exchange.start()
+            exchanges.append((group, exchange))
 
     for half in range(HALVES):
         wait_bytes(send_a.at[half, others], a_send.at[half])
@@ -356,8 +411,10 @@
     wait_bytes(seven, w1_send)
     wait_bytes(weights.at[pl.ds(0, 3)], w2_send)
     wait_bytes(weights.at[pl.ds(0, 4)], w3_send)
-    exchange.wait()
-    out_ref[...] = (acc[0] + part_in[...].astype(F32)).astype(BF16)
+    for group, exchange in exchanges:
+        tokens = tokens_of(group)
+        exchange.wait()
+        out_ref[tokens] = (acc[0, tokens] + part_in[tokens].astype(F32)).astype(BF16)
 
 
 def per_device(key_value, gating, long_filter, skip_gain, out_weight):
@@ -368,9 +425,18 @@
     return pl.pallas_call(
         kernel,
         out_shape=jax.ShapeDtypeStruct((TOK, CH), BF16),
-        in_specs=[vmem, vmem, vmem, vmem, anywhere, vmem, vmem, vmem, vmem],
+        in_specs=[anywhere] * 9,
         out_specs=vmem,
         scratch_shapes=[
+            pltpu.VMEM((TOK, CH), BF16),
+            pltpu.VMEM((TOK, CH), BF16),
+            pltpu.VMEM((TOK, CH), BF16),
+            pltpu.VMEM((1, CH), F32),
+            pltpu.VMEM((128, 256), BF16),
+            pltpu.VMEM((256, 128), BF16),
+            pltpu.VMEM((128, 256), BF16),
+            pltpu.VMEM((256, 256), BF16),
+            dma((8,)),
             pltpu.VMEM((HALVES, SEQ * ROWS, LANES), F32),
             pltpu.VMEM((HALVES, SEQ, 2 * ROWS, LANES), BF16),
             pltpu.VMEM((HALVES, SEQ, 2 * ROWS, LANES), BF16),
@@ -388,10 +454,10 @@
             dma((HALVES,)), dma((HALVES,)), dma((HALVES,)), dma((HALVES,)),
             dma, dma, dma, dma, dma, dma, dma((2,)),
             ring, ring, ring, ring,
-            dma, dma,
+            dma((GROUPS,)), dma((GROUPS,)),
         ],
         compiler_params=pltpu.CompilerParams(
-            collective_id=0, has_side_effects=True, vmem_limit_bytes=48 * 2**20
+            collective_id=0, has_side_effects=True, vmem_limit_bytes=60 * 2**20
         ),
     )(
         key_value, gating, long_filter, skip_gain.reshape(1, CH), out_weight,

time: 95.3 us -> 79.8 us (0.84)
  the two profiles are of different devices: /device:TPU:8 before, /device:TPU:2 now
where the time goes in v2:
time: 79.8 us; the launch traced here: 79.6 us
  Pallas kernels  77.9 us (98%)
  local copies, waits for them, and re-layouts  1.67 us (2%)
    pallas_call x1, Pallas kernels, per_device(): pl.pallas_call(kernel, out_shape=jax.ShapeDtypeStruct((TOK, CH), BF16), i...  77.9 us
    unnamed x1, local copies, waits for them, and re-layouts  1.67 us

profile of v2, /device:TPU:2, one launch (start us, length us, event | category | flops | bytes accessed | tf_op | source)
XLA Modules:
  0.0 79.6 jit_solution(2813395843932120700)
XLA Ops:
  0.0 77.9 %shard_map.91 = bf16[512,256]{1,0:T(8,128)(2,1)} custom-call(bf16[512,256]{1,0:T(8,128)(2,1)} %kv_hbm.1, bf16[512,256]{1,0:T(8,128)(2,1)} %gate_hbm.1, bf16[512,256]{1,0:T(8,128)(2,1)} %filt_hbm.1, f32[1,256]{1,0:T(1,128)} %bitcast.1, bf16[256,4096]{1,0:T(8,128)(2,1)} %w_ref.1, bf16[128,256]{1,0:T(8,128)(2,1)} %constant.6.clone.to_lane_hbm.from_row_hbm, ...), custom_call_target="tpu_custom_call" | custom-call | tf_op jit(solution)/shard_map/pallas_call | solution.py:425
  77.9 1.7 %copy.11 = bf16[512,256]{1,0:T(8,128)(2,1)} copy(bf16[512,256]{1,0:T(8,128)(2,1)} %shard_map.91) | data formatting | bytes 524288

commit v3 on v2

--- a/solution.py
+++ b/solution.py
@@ -27,11 +27,13 @@
 GROUPS = 2
 GROUP = TOK // GROUPS
 ORDER = (
-    (0, 0, 1), (0, 1, 1), (1, 0, 0), (0, 0, 2), (0, 1, 2), (1, 0, 1), (1, 1, -1), (0, 0, 3), (0, 1, 3),
-    (1, 0, 2), (1, 1, 0), (1, 0, 3), (1, 1, 1), (1, 1, 2), (1, 1, 3),
+    ("conv", 0), ("gate", 0), ("start", 0, 0), ("start", 0, 1), ("conv", 1), ("step", 0, 0, 0), ("step", 0, 1, 0),
+    ("legs",), ("gate", 1), ("start", 1, 0), ("step", 0, 0, 1), ("step", 0, 1, 1), ("weights",), ("start", 1, 1),
+    ("step", 1, 0, 0), ("step", 0, 0, 2), ("step", 0, 1, 2), ("step", 1, 0, 1), ("step", 1, 1, 0), ("step", 0, 0, 3),
+    ("step", 0, 1, 3), ("step", 1, 0, 2), ("step", 1, 1, 1), ("step", 1, 0, 3), ("step", 1, 1, 2), ("step", 1, 1, 3),
 )
-SHARE = 32
-SHARES = CH // SHARE
+SHARES = (8, 2)
+SERIAL = True
 
 
 def tables():
@@ -66,7 +68,7 @@
     out_ref,
     kv_ref, gate_ref, filt_ref, skip_ref, to_lane, to_row, from_row, from_lane, load_sem,
     spread, send_a, recv_a, rows_x, rows_h, rows_y, send_c, recv_c, rows_c,
-    gated, weights, acc, part_out, part_in,
+    gated, weights_0, weights_1, acc, part_out, part_in,
     a_send, a_recv, c_send, c_recv, w1_send, w1_recv, w2_send, w2_recv, w3_send, w3_recv, w_local,
     right_send, right_recv, left_send, left_recv, y_send, y_recv,
 ):
@@ -76,7 +78,17 @@
     z = lax.rem(chan, Z)
     core = lax.rem(me, 2)
     x = me // 8
-    share = x * 2 + core
+    shares = [x * 2 + core if SHARES[half] == 8 else core for half in range(HALVES)]
+    weights = (weights_0, weights_1)
+    depths = [CHUNK_CH // SHARES[half] for half in range(HALVES)]
+
+    def weight_piece(half, to, rel):
+        row = half * CHUNK_CH + shares[half] * depths[half]
+        column = (y_hi + rel - 2 * y_hi * rel) * Z * CH + to * CH
+        return w_ref.at[
+            pl.ds(pl.multiple_of(row, depths[half]), depths[half]), pl.ds(pl.multiple_of(column, CH), CH)
+        ]
+
 
     def chan_of(hi, zz):
         return hi * Z + lax.rem(zz, Z)
@@ -135,15 +147,9 @@
 
     own_copies = [
         pltpu.make_async_copy(
-            w_ref.at[
-                pl.ds(pl.multiple_of(share * SHARE, SHARE), SHARE),
-                pl.ds(
-                    pl.multiple_of((y_hi + rel - 2 * y_hi * rel) * Z * CH + z * CH, CH), CH
-                ),
-            ],
-            weights.at[share, z, rel],
-            w_local.at[rel],
-        )
+            weight_piece(half, z, rel), weights[half].at[shares[half], z, rel], w_local.at[half, rel]
+        )
+        for half in range(HALVES)
         for rel in range(2)
     ]
     for copy in own_copies:
@@ -173,26 +179,27 @@
     def wait_bytes(ref, sem):
         pltpu.make_async_copy(ref, ref, sem).wait()
 
-    def send_weight(k, carry):
-        to = lax.rem(z + k, Z)
-        for rel in range(2):
-            column = (y_hi + rel - 2 * y_hi * rel) * Z * CH + to * CH
-            pltpu.make_async_remote_copy(
-                src_ref=w_ref.at[
-                    pl.ds(pl.multiple_of(share * SHARE, SHARE), SHARE),
-                    pl.ds(pl.multiple_of(column, CH), CH),
-                ],
-                dst_ref=weights.at[share, z, rel],
-                send_sem=w1_send,
-                recv_sem=w1_recv,
-                device_id={"chan": chan_of(y_hi, to)},
-                device_id_type=MESH,
-            ).start()
-        return carry
-
-    lax.fori_loop(1, Z, send_weight, 0)
     for half in range(HALVES):
-        send_signal(half)
+
+        def send_weight(k, carry, half=half):
+            to = lax.rem(z + k, Z)
+            for rel in range(2):
+                pltpu.make_async_remote_copy(
+                    src_ref=weight_piece(half, to, rel),
+                    dst_ref=weights[half].at[shares[half], z, rel],
+                    send_sem=w1_send.at[half],
+                    recv_sem=w1_recv.at[half],
+                    device_id={"chan": chan_of(y_hi, to)},
+                    device_id_type=MESH,
+                ).start()
+            return carry
+
+        lax.fori_loop(1, Z, send_weight, 0)
+    others = pl.ds(0, SEQ - 1)
+    send_signal(0)
+    if SERIAL:
+        wait_bytes(send_a.at[0, others], a_send.at[0])
+    send_signal(1)
 
     def convolve(half):
         rows_x[...] = recv_a[half, :, :ROWS, :].astype(F32).reshape(SEQ * ROWS, LANES)
@@ -229,36 +236,54 @@
 
         lax.fori_loop(1, SEQ, one, 0)
 
-    others = pl.ds(0, SEQ - 1)
-
-    def second_leg(k, carry):
-        peer = lax.rem(me + 8 * k, SEQ)
-        pltpu.make_async_remote_copy(
-            src_ref=weights.at[share],
-            dst_ref=weights.at[share],
-            send_sem=w2_send,
-            recv_sem=w2_recv,
-            device_id={"seq": peer},
-            device_id_type=MESH,
-        ).start()
-        return carry
-
-    def third_leg(k, carry):
-        which = 2 * k + core
-        pltpu.make_async_remote_copy(
-            src_ref=weights.at[which],
-            dst_ref=weights.at[which],
-            send_sem=w3_send,
-            recv_sem=w3_recv,
-            device_id={"seq": me + 1 - 2 * core},
-            device_id_type=MESH,
-        ).start()
-        return carry
-
-    seven = weights.at[0, pl.ds(0, Z - 1)]
-    wait_bytes(seven, w1_recv)
-    lax.fori_loop(1, 4, second_leg, 0)
+    def first_leg_bytes(half):
+        return weights[half].at[0, pl.ds(0, Z - 1)]
+
+    def second_leg(half):
+        if SHARES[half] == 2:
+            return
+        share = shares[half]
+
+        def one(k, carry):
+            pltpu.make_async_remote_copy(
+                src_ref=weights[half].at[share],
+                dst_ref=weights[half].at[share],
+                send_sem=w2_send.at[half],
+                recv_sem=w2_recv.at[half],
+                device_id={"seq": lax.rem(me + 8 * k, SEQ)},
+                device_id_type=MESH,
+            ).start()
+            return carry
+
+        wait_bytes(first_leg_bytes(half), w1_recv.at[half])
+        lax.fori_loop(1, 4, one, 0)
+
+    def third_leg(half):
+        if SHARES[half] == 2:
+            wait_bytes(first_leg_bytes(half), w1_recv.at[half])
+        else:
+            wait_bytes(weights[half].at[pl.ds(0, 3)], w2_recv.at[half])
+
+        def one(k, carry):
+            which = 2 * k + core
+            pltpu.make_async_remote_copy(
+                src_ref=weights[half].at[which],
+                dst_ref=weights[half].at[which],
+                send_sem=w3_send.at[half],
+                recv_sem=w3_recv.at[half],
+                device_id={"seq": me + 1 - 2 * core},
+                device_id_type=MESH,
+            ).start()
+            return carry
+
+        lax.fori_loop(0, SHARES[half] // 2, one, 0)
+
+    def third_leg_bytes(half):
+        return weights[half].at[pl.ds(0, SHARES[half] // 2)]
+
     for half in range(HALVES):
+        second_leg(half)
+    def transform(half):
         wait_bytes(recv_a.at[half, others], a_recv.at[half])
         convolve(half)
         send_back(half)
@@ -305,10 +330,9 @@
         return range(group * per, (group + 1) * per)
 
     def add_block(block, half, group, first=False):
-        shares = CHUNK_CH // SHARE
         tokens = tokens_of(group)
         for rel in range(2):
-            weight = weights[half * shares : (half + 1) * shares, block, rel].reshape(CHUNK_CH, CH)
+            weight = weights[half][:, block, rel].reshape(CHUNK_CH, CH)
             term = dot(gated[block, half, tokens], weight)
             if first:
                 acc[rel, tokens] = term
@@ -363,44 +387,55 @@
         if step < 3:
             add_block(from_right, half, group)
 
-    gate(0)
-    for group in range(GROUPS):
-        start_group(0, group)
-    wait_bytes(weights.at[pl.ds(0, 3)], w2_recv)
-    lax.fori_loop(0, 4, third_leg, 0)
-    for group in range(GROUPS):
-        pass_on(0, group, 0)
-    gate(1)
-    start_group(1, 0)
-    wait_bytes(weights.at[pl.ds(0, 4)], w3_recv)
-    for group in range(GROUPS):
-        add_block(z, 0, group, True)
-        add_block(z, 1, group)
-        add_step(0, group, 0)
-
     exchanges = []
-    for half, group, step in ORDER:
-        if step < 0:
-            start_group(half, group)
-            continue
-        pass_on(half, group, step)
+    waiting = []
+
+    def finish(half, group, step):
         add_step(half, group, step)
-        if half == HALVES - 1 and step == 3:
-            tokens = tokens_of(group)
-            part_out[tokens] = acc[1, tokens].astype(BF16)
-            exchange = pltpu.make_async_remote_copy(
-                src_ref=part_out.at[tokens],
-                dst_ref=part_in.at[tokens],
-                send_sem=y_send.at[group],
-                recv_sem=y_recv.at[group],
-                device_id={"chan": partner},
-                device_id_type=MESH,
-            )
-            exchange.start()
-            exchanges.append((group, exchange))
+        if half < HALVES - 1 or step < 3:
+            return
+        tokens = tokens_of(group)
+        part_out[tokens] = acc[1, tokens].astype(BF16)
+        exchange = pltpu.make_async_remote_copy(
+            src_ref=part_out.at[tokens],
+            dst_ref=part_in.at[tokens],
+            send_sem=y_send.at[group],
+            recv_sem=y_recv.at[group],
+            device_id={"chan": partner},
+            device_id_type=MESH,
+        )
+        exchange.start()
+        exchanges.append((group, exchange))
+
+    for kind, *event in ORDER:
+        if kind == "conv":
+            transform(*event)
+        elif kind == "start":
+            start_group(*event)
+        elif kind == "legs":
+            for half in range(HALVES):
+                third_leg(half)
+        elif kind == "gate":
+            gate(*event)
+        elif kind == "weights":
+            for half in range(HALVES):
+                wait_bytes(third_leg_bytes(half), w3_recv.at[half])
+            for group in range(GROUPS):
+                add_block(z, 0, group, True)
+                add_block(z, 1, group)
+            for arrived in waiting:
+                finish(*arrived)
+            waiting = None
+        else:
+            pass_on(*event)
+            if waiting is None:
+                finish(*event)
+            else:
+                waiting.append(event)
 
     for half in range(HALVES):
-        wait_bytes(send_a.at[half, others], a_send.at[half])
+        if half > 0 or not SERIAL:
+            wait_bytes(send_a.at[half, others], a_send.at[half])
         wait_bytes(send_c.at[half, others], c_send.at[half])
         for step in range(4):
             for chunk in range(TOK_CHUNKS):
@@ -408,9 +443,11 @@
                     arrive(piece(0, half, chunk), right_send.at[half, step, chunk])
                 if goes_left(step, chunk):
                     arrive(piece(0, half, chunk), left_send.at[half, step, chunk])
-    wait_bytes(seven, w1_send)
-    wait_bytes(weights.at[pl.ds(0, 3)], w2_send)
-    wait_bytes(weights.at[pl.ds(0, 4)], w3_send)
+    for half in range(HALVES):
+        wait_bytes(first_leg_bytes(half), w1_send.at[half])
+        if SHARES[half] == 8:
+            wait_bytes(weights[half].at[pl.ds(0, 3)], w2_send.at[half])
+        wait_bytes(third_leg_bytes(half), w3_send.at[half])
     for group, exchange in exchanges:
         tokens = tokens_of(group)
         exchange.wait()
@@ -447,12 +484,12 @@
             pltpu.VMEM((HALVES, SEQ, ROWS, LANES), BF16),
             pltpu.VMEM((SEQ * ROWS, LANES), F32),
             pltpu.VMEM((Z, HALVES, TOK, CHUNK_CH), BF16),
-            pltpu.VMEM((SHARES, Z, 2, SHARE, CH), BF16),
+            *(pltpu.VMEM((count, Z, 2, CHUNK_CH // count, CH), BF16) for count in SHARES),
             pltpu.VMEM((2, TOK, CH), F32),
             pltpu.VMEM((TOK, CH), BF16),
             pltpu.VMEM((TOK, CH), BF16),
             dma((HALVES,)), dma((HALVES,)), dma((HALVES,)), dma((HALVES,)),
-            dma, dma, dma, dma, dma, dma, dma((2,)),
+            *(dma((HALVES,)) for _ in range(6)), dma((HALVES, 2)),
             ring, ring, ring, ring,
             dma((GROUPS,)), dma((GROUPS,)),
         ],

time: 79.8 us -> 74.1 us (0.929)
  the two profiles are of different devices: /device:TPU:2 before, /device:TPU:24 now
where the time goes in v3:
time: 74.1 us; the launch traced here: 73.9 us
  Pallas kernels  72.2 us (97%)
  local copies, waits for them, and re-layouts  1.67 us (2%)
    pallas_call x1, Pallas kernels, per_device(): pl.pallas_call(kernel, out_shape=jax.ShapeDtypeStruct((TOK, CH), BF16), i...  72.2 us
    unnamed x1, local copies, waits for them, and re-layouts  1.67 us

profile of v3, /device:TPU:24, one launch (start us, length us, event | category | flops | bytes accessed | tf_op | source)
XLA Modules:
  0.0 73.9 jit_solution(17767463788354871348)
XLA Ops:
  0.0 72.2 %shard_map.91 = bf16[512,256]{1,0:T(8,128)(2,1)} custom-call(bf16[512,256]{1,0:T(8,128)(2,1)} %kv_hbm.1, bf16[512,256]{1,0:T(8,128)(2,1)} %gate_hbm.1, bf16[512,256]{1,0:T(8,128)(2,1)} %filt_hbm.1, f32[1,256]{1,0:T(1,128)} %bitcast.1, bf16[256,4096]{1,0:T(8,128)(2,1)} %w_ref.1, bf16[128,256]{1,0:T(8,128)(2,1)} %constant.6.clone.to_lane_hbm.from_row_hbm, ...), custom_call_target="tpu_custom_call" | custom-call | tf_op jit(solution)/shard_map/pallas_call | solution.py:462
  72.2 1.7 %copy.11 = bf16[512,256]{1,0:T(8,128)(2,1)} copy(bf16[512,256]{1,0:T(8,128)(2,1)} %shard_map.91) | data formatting | bytes 524288

commit v4 on v3

--- a/solution.py
+++ b/solution.py
@@ -27,13 +27,13 @@
 GROUPS = 2
 GROUP = TOK // GROUPS
 ORDER = (
-    ("conv", 0), ("gate", 0), ("start", 0, 0), ("start", 0, 1), ("conv", 1), ("step", 0, 0, 0), ("step", 0, 1, 0),
-    ("legs",), ("gate", 1), ("start", 1, 0), ("step", 0, 0, 1), ("step", 0, 1, 1), ("weights",), ("start", 1, 1),
-    ("step", 1, 0, 0), ("step", 0, 0, 2), ("step", 0, 1, 2), ("step", 1, 0, 1), ("step", 1, 1, 0), ("step", 0, 0, 3),
-    ("step", 0, 1, 3), ("step", 1, 0, 2), ("step", 1, 1, 1), ("step", 1, 0, 3), ("step", 1, 1, 2), ("step", 1, 1, 3),
+    ("conv", 0), ("conv", 1), ("gate", 0), ("start", 0, 0), ("legs",), ("gate", 1), ("start", 1, 0), ("step", 0, 0, 0),
+    ("step", 1, 0, 0), ("weights",), ("step", 0, 0, 1), ("step", 1, 0, 1), ("start", 0, 1), ("start", 1, 1),
+    ("step", 0, 0, 2), ("step", 1, 0, 2), ("step", 0, 1, 0), ("step", 1, 1, 0), ("step", 0, 0, 3), ("step", 1, 0, 3),
+    ("step", 0, 1, 1), ("step", 1, 1, 1), ("step", 0, 1, 2), ("step", 1, 1, 2), ("step", 0, 1, 3), ("step", 1, 1, 3),
 )
 SHARES = (8, 2)
-SERIAL = True
+WEIGHTS_FIRST = True
 
 
 def tables():
@@ -139,11 +139,11 @@
                         quarter * SEQ : (quarter + 1) * SEQ
                     ]
         for half in range(HALVES):
-            send_a[half, :, which * ROWS : (which + 1) * ROWS, :] = (
+            at = (2 * half + which) * ROWS
+            send_a[:, at : at + ROWS, :] = (
                 spread[half].reshape(SEQ, ROWS, LANES).astype(BF16)
             )
-    for half in range(HALVES):
-        recv_a[half, me] = send_a[half, me]
+    recv_a[me] = send_a[me]
 
     own_copies = [
         pltpu.make_async_copy(
@@ -161,14 +161,14 @@
         copy.wait()
     pl.semaphore_wait(barrier, SEQ - 1 + Z - 1 + 1)
 
-    def send_signal(half):
+    def send_signal():
         def one(k, carry):
             peer = lax.rem(me + k, SEQ)
             pltpu.make_async_remote_copy(
-                src_ref=send_a.at[half, peer],
-                dst_ref=recv_a.at[half, me],
-                send_sem=a_send.at[half],
-                recv_sem=a_recv.at[half],
+                src_ref=send_a.at[peer],
+                dst_ref=recv_a.at[me],
+                send_sem=a_send,
+                recv_sem=a_recv,
                 device_id={"seq": peer},
                 device_id_type=MESH,
             ).start()
@@ -179,6 +179,8 @@
     def wait_bytes(ref, sem):
         pltpu.make_async_copy(ref, ref, sem).wait()
 
+    if not WEIGHTS_FIRST:
+        send_signal()
     for half in range(HALVES):
 
         def send_weight(k, carry, half=half):
@@ -196,14 +198,13 @@
 
         lax.fori_loop(1, Z, send_weight, 0)
     others = pl.ds(0, SEQ - 1)
-    send_signal(0)
-    if SERIAL:
-        wait_bytes(send_a.at[0, others], a_send.at[0])
-    send_signal(1)
+    if WEIGHTS_FIRST:
+        send_signal()
 
     def convolve(half):
-        rows_x[...] = recv_a[half, :, :ROWS, :].astype(F32).reshape(SEQ * ROWS, LANES)
-        rows_h[...] = recv_a[half, :, ROWS:, :].astype(F32).reshape(SEQ * ROWS, LANES)
+        for which, rows in enumerate((rows_x, rows_h)):
+            at = (2 * half + which) * ROWS
+            rows[...] = recv_a[:, at : at + ROWS, :].astype(F32).reshape(SEQ * ROWS, LANES)
         first_row = lax.broadcasted_iota(jnp.int32, (LANES, LANES), 0) == 0
         for own in range(OWN):
             spectra = []
@@ -284,7 +285,8 @@
     for half in range(HALVES):
         second_leg(half)
     def transform(half):
-        wait_bytes(recv_a.at[half, others], a_recv.at[half])
+        if half == 0:
+            wait_bytes(recv_a.at[others], a_recv)
         convolve(half)
         send_back(half)
 
@@ -433,9 +435,8 @@
             else:
                 waiting.append(event)
 
+    wait_bytes(send_a.at[others], a_send)
     for half in range(HALVES):
-        if half > 0 or not SERIAL:
-            wait_bytes(send_a.at[half, others], a_send.at[half])
         wait_bytes(send_c.at[half, others], c_send.at[half])
         for step in range(4):
             for chunk in range(TOK_CHUNKS):
@@ -475,8 +476,8 @@
             pltpu.VMEM((256, 256), BF16),
             dma((8,)),
             pltpu.VMEM((HALVES, SEQ * ROWS, LANES), F32),
-            pltpu.VMEM((HALVES, SEQ, 2 * ROWS, LANES), BF16),
-            pltpu.VMEM((HALVES, SEQ, 2 * ROWS, LANES), BF16),
+            pltpu.VMEM((SEQ, HALVES * 2 * ROWS, LANES), BF16),
+            pltpu.VMEM((SEQ, HALVES * 2 * ROWS, LANES), BF16),
             pltpu.VMEM((SEQ * ROWS, LANES), F32),
             pltpu.VMEM((SEQ * ROWS, LANES), F32),
             pltpu.VMEM((SEQ * ROWS, LANES), F32),
@@ -488,7 +489,7 @@
             pltpu.VMEM((2, TOK, CH), F32),
             pltpu.VMEM((TOK, CH), BF16),
             pltpu.VMEM((TOK, CH), BF16),
-            dma((HALVES,)), dma((HALVES,)), dma((HALVES,)), dma((HALVES,)),
+            dma, dma, dma((HALVES,)), dma((HALVES,)),
             *(dma((HALVES,)) for _ in range(6)), dma((HALVES, 2)),
             ring, ring, ring, ring,
             dma((GROUPS,)), dma((GROUPS,)),

time: 74.1 us -> 73 us (0.985)
  the two profiles are of different devices: /device:TPU:24 before, /device:TPU:2 now
where the time goes in v4:
time: 73 us; the launch traced here: 72.8 us
  Pallas kernels  71.1 us (97%)
  local copies, waits for them, and re-layouts  1.67 us (2%)
    pallas_call x1, Pallas kernels, per_device(): pl.pallas_call(kernel, out_shape=jax.ShapeDtypeStruct((TOK, CH), BF16), i...  71.1 us
    unnamed x1, local copies, waits for them, and re-layouts  1.67 us

profile of v4, /device:TPU:2, one launch (start us, length us, event | category | flops | bytes accessed | tf_op | source)
XLA Modules:
  0.0 72.8 jit_solution(17638909593911606634)
XLA Ops:
  0.0 71.1 %shard_map.91 = bf16[512,256]{1,0:T(8,128)(2,1)} custom-call(bf16[512,256]{1,0:T(8,128)(2,1)} %kv_hbm.1, bf16[512,256]{1,0:T(8,128)(2,1)} %gate_hbm.1, bf16[512,256]{1,0:T(8,128)(2,1)} %filt_hbm.1, f32[1,256]{1,0:T(1,128)} %bitcast.1, bf16[256,4096]{1,0:T(8,128)(2,1)} %w_ref.1, bf16[128,256]{1,0:T(8,128)(2,1)} %constant.6.clone.to_lane_hbm.from_row_hbm, ...), custom_call_target="tpu_custom_call" | custom-call | tf_op jit(solution)/shard_map/pallas_call | solution.py:463
  71.1 1.7 %copy.11 = bf16[512,256]{1,0:T(8,128)(2,1)} copy(bf16[512,256]{1,0:T(8,128)(2,1)} %shard_map.91) | data formatting | bytes 524288

commit v5 on v4

--- a/solution.py
+++ b/solution.py
@@ -25,7 +25,7 @@
 TOK_CHUNKS = 4
 PIECE = TOK // TOK_CHUNKS
 GROUPS = 2
-GROUP = TOK // GROUPS
+FIRST = 3
 ORDER = (
     ("conv", 0), ("conv", 1), ("gate", 0), ("start", 0, 0), ("legs",), ("gate", 1), ("start", 1, 0), ("step", 0, 0, 0),
     ("step", 1, 0, 0), ("weights",), ("step", 0, 0, 1), ("step", 1, 0, 1), ("start", 0, 1), ("start", 1, 1),
@@ -324,12 +324,12 @@
     def goes_left(step, chunk):
         return step < 3 or (step == 3 and chunk % 2 == 1)
 
+    def chunks_of(group):
+        return range(FIRST) if group == 0 else range(FIRST, TOK_CHUNKS)
+
     def tokens_of(group):
-        return pl.ds(group * GROUP, GROUP)
-
-    def chunks_of(group):
-        per = TOK_CHUNKS // GROUPS
-        return range(group * per, (group + 1) * per)
+        chunks = chunks_of(group)
+        return pl.ds(chunks[0] * PIECE, len(chunks) * PIECE)
 
     def add_block(block, half, group, first=False):
         tokens = tokens_of(group)

time: 73 us -> 73.8 us (1.011)
  the two profiles are of different devices: /device:TPU:2 before, /device:TPU:16 now
where the time goes in v5:
time: 73.8 us; the launch traced here: 73.6 us
  Pallas kernels  71.9 us (97%)
  local copies, waits for them, and re-layouts  1.67 us (2%)
    pallas_call x1, Pallas kernels, per_device(): pl.pallas_call(kernel, out_shape=jax.ShapeDtypeStruct((TOK, CH), BF16), i...  71.9 us
    unnamed x1, local copies, waits for them, and re-layouts  1.67 us

profile of v5, /device:TPU:16, one launch (start us, length us, event | category | flops | bytes accessed | tf_op | source)
XLA Modules:
  0.0 73.6 jit_solution(7542069578960945199)
XLA Ops:
  0.0 71.9 %shard_map.91 = bf16[512,256]{1,0:T(8,128)(2,1)} custom-call(bf16[512,256]{1,0:T(8,128)(2,1)} %kv_hbm.1, bf16[512,256]{1,0:T(8,128)(2,1)} %gate_hbm.1, bf16[512,256]{1,0:T(8,128)(2,1)} %filt_hbm.1, f32[1,256]{1,0:T(1,128)} %bitcast.1, bf16[256,4096]{1,0:T(8,128)(2,1)} %w_ref.1, bf16[128,256]{1,0:T(8,128)(2,1)} %constant.6.clone.to_lane_hbm.from_row_hbm, ...), custom_call_target="tpu_custom_call" | custom-call | tf_op jit(solution)/shard_map/pallas_call | solution.py:463
  71.9 1.7 %copy.11 = bf16[512,256]{1,0:T(8,128)(2,1)} copy(bf16[512,256]{1,0:T(8,128)(2,1)} %shard_map.91) | data formatting | bytes 524288
